TPU v7x, 512 devices: a whole 4x4x16 slice. The times are simulated.
512 devices in a mesh: dp: 8 (over y, core), seq: 64 (over x, z).
Axes of the slice: x: 4, y: 4, z: 16, core: 2. Of those that a mesh axis runs over, the one named last changes fastest.
Arguments:
- queries: bfloat16 [8, 16384, 384], P('dp', 'seq'), may hold values from -6 to 6
- keys: bfloat16 [8, 16384, 384], P('dp', 'seq'), may hold values from -6 to 6
- values: bfloat16 [8, 16384, 384], P('dp', 'seq'), may hold values from -6 to 6
- outputs: bfloat16 [8, 16384, 384], P('dp', 'seq'), may hold values from -16 to 16
- d_final: bfloat16 [8, 16384, 768], P('dp', 'seq'), may hold values from -6 to 6
- stats: float32 [8, 16384, 8], P('dp', 'seq'), may hold values from 6.5 to 8
- w_out: bfloat16 [384, 768], replicated, may hold values from -0.21875 to 0.21875
Outputs:
- d_queries: bfloat16 [8, 16384, 384], P('dp', 'seq')
- d_keys: bfloat16 [8, 16384, 384], P('dp', 'seq')
- d_values: bfloat16 [8, 16384, 384], P('dp', 'seq')
- grad_weight: float32 [384, 768], P('seq')
All inputs are finite; a program needn't handle non-finite values.
Results may differ from a plain program's by a relative error of at most 0.0057.
Values may be sent and summed in bfloat16 or wider, within the bound.
No kernel may reach another device: no remote copies, remote signals or barrier semaphores. Data moves between devices by JAX's collectives and lax.ppermute only.
A program may use at most 64 MiB of HBM per device.

v0:
```python
import jax
import jax.numpy as jnp
from jax import lax
from jax.sharding import PartitionSpec as P

GROUP = 8


def swapped(shard, axis, distance):
    return lax.ppermute(shard, axis, [(i, i ^ 1 << distance) for i in range(lax.axis_size(axis))])


def pick(x, stride, heads):
    shaped = x.reshape(x.shape[0] // stride, stride, heads, x.shape[-1])
    return jnp.stack([shaped[:, h % stride, h, :] for h in range(heads)], axis=1)


def place(y, stride, heads, rows):
    shaped = jnp.zeros((rows // stride, stride, heads, y.shape[-1]), jnp.float32)
    for h in range(heads):
        shaped = shaped.at[:, h % stride, h, :].set(y[:, h, :])
    return shaped.reshape(rows, heads, y.shape[-1])


def set_backward(query, d_out, lse, delta, keys, values, scale):
    scores = jnp.einsum("nhc,mhc->hnm", query, keys, preferred_element_type=jnp.float32) * scale
    probs = jnp.exp(scores - jnp.transpose(lse)[:, :, None])
    d_probs = jnp.einsum("nhc,mhc->hnm", d_out, values, preferred_element_type=jnp.float32)
    d_scores = (probs * (d_probs - jnp.transpose(delta)[:, :, None])).astype(jnp.bfloat16)
    probs_low = probs.astype(jnp.bfloat16)
    d_query = jnp.einsum("hnm,mhc->nhc", d_scores, keys, preferred_element_type=jnp.float32) * scale
    d_key = jnp.einsum("hnm,nhc->mhc", d_scores, query, preferred_element_type=jnp.float32) * scale
    d_value = jnp.einsum("hnm,nhc->mhc", probs_low, d_out, preferred_element_type=jnp.float32)
    return (d_query, d_key, d_value)


def group_collect(block, bits):
    where = lax.axis_index("seq")
    gathered = block
    for bit in range(bits):
        other = swapped(gathered, "seq", bit)
        high = where >> bit & 1
        gathered = jnp.where(
            high == 1,
            jnp.concatenate([other, gathered], axis=1),
            jnp.concatenate([gathered, other], axis=1),
        )
    return gathered


def group_return(grads, bits):
    where = lax.axis_index("seq")
    current = grads
    for bit in reversed(range(bits)):
        half = current.shape[1] // 2
        lower = current[:, :half]
        upper = current[:, half:]
        high = where >> bit & 1
        keep = jnp.where(high == 1, upper, lower)
        send = jnp.where(high == 1, lower, upper)
        current = keep + swapped(send, "seq", bit)
    return current


def on_device(queries, keys, values, outputs, d_final, stats, w_out):
    query2 = queries[0]
    key2 = keys[0]
    value2 = values[0]
    output2 = outputs[0]
    upstream = d_final[0]
    lse = stats[0]
    rows = query2.shape[0]
    width = query2.shape[1]
    heads = lse.shape[1]
    size = width // heads
    scale = float(size) ** (-0.5)
    seq_count = lax.axis_size("seq")
    d_out = lax.dot_general(
        upstream, w_out, (((1,), (1,)), ((), ())), preferred_element_type=jnp.float32
    ).astype(jnp.bfloat16)
    query3 = query2.reshape(rows, heads, size)
    key3 = key2.reshape(rows, heads, size)
    value3 = value2.reshape(rows, heads, size)
    dout3 = d_out.reshape(rows, heads, size)
    delta = jnp.sum(
        dout3.astype(jnp.float32) * output2.reshape(rows, heads, size).astype(jnp.float32), axis=-1
    )
    full = lax.dot_general(
        output2, upstream, (((0,), (0,)), ((), ())), preferred_element_type=jnp.float32
    )
    summed = lax.psum(full, "dp")
    grad_weight = lax.psum_scatter(summed, "seq", scatter_dimension=0, tiled=True)
    dq0, dk0, dv0 = set_backward(query3, dout3, lse, delta, key3, value3, scale)
    total_q = dq0
    total_k = dk0
    total_v = dv0

    def level_inputs(stride):
        return (
            pick(query3, stride, heads),
            pick(dout3, stride, heads),
            pick(lse[:, :, None], stride, heads)[..., 0],
            pick(delta[:, :, None], stride, heads)[..., 0],
            pick(key3, stride, heads),
            pick(value3, stride, heads),
        )

    group_bits = GROUP.bit_length() - 1
    pq, pd, pl, pdl, pk, pv = level_inputs(GROUP)
    count = rows // GROUP
    pair = jnp.stack([pk.reshape(count, width), pv.reshape(count, width)])
    remote = group_collect(pair, group_bits)
    dq1, dk1, dv1 = set_backward(
        pq,
        pd,
        pl,
        pdl,
        remote[0].reshape(-1, heads, size),
        remote[1].reshape(-1, heads, size),
        scale,
    )
    back = group_return(jnp.stack([dk1.reshape(-1, width), dv1.reshape(-1, width)]), group_bits)
    total_q = total_q + place(dq1, GROUP, heads, rows)
    total_k = total_k + place(back[0].reshape(count, heads, size), GROUP, heads, rows)
    total_v = total_v + place(back[1].reshape(count, heads, size), GROUP, heads, rows)
    fq, fd, fl, fdl, fk, fv = level_inputs(seq_count)
    far_count = rows // seq_count
    far_pair = jnp.stack([fk.reshape(far_count, width), fv.reshape(far_count, width)])
    far_remote = lax.all_gather(far_pair, "seq", axis=1, tiled=True)
    dq2, dk2, dv2 = set_backward(
        fq,
        fd,
        fl,
        fdl,
        far_remote[0].reshape(-1, heads, size),
        far_remote[1].reshape(-1, heads, size),
        scale,
    )
    far_terms = jnp.stack([dk2.reshape(-1, width), dv2.reshape(-1, width)])
    far_back = lax.psum_scatter(far_terms, "seq", scatter_dimension=1, tiled=True)
    total_q = total_q + place(dq2, seq_count, heads, rows)
    total_k = total_k + place(far_back[0].reshape(far_count, heads, size), seq_count, heads, rows)
    total_v = total_v + place(far_back[1].reshape(far_count, heads, size), seq_count, heads, rows)
    d_queries = total_q.reshape(1, rows, width).astype(jnp.bfloat16)
    d_keys = total_k.reshape(1, rows, width).astype(jnp.bfloat16)
    d_values = total_v.reshape(1, rows, width).astype(jnp.bfloat16)
    return (d_queries, d_keys, d_values, grad_weight)


def solution(mesh):
    placed = (
        P("dp", "seq", None),
        P("dp", "seq", None),
        P("dp", "seq", None),
        P("dp", "seq", None),
        P("dp", "seq", None),
        P("dp", "seq", None),
        P(),
    )
    return jax.shard_map(
        on_device,
        mesh=mesh,
        in_specs=placed,
        out_specs=(
            P("dp", "seq", None),
            P("dp", "seq", None),
            P("dp", "seq", None),
            P("seq", None),
        ),
        check_vma=False,
    )
```

profile of v0, /device:TPU:8, one launch (start us, length us, event | category | flops | bytes accessed | tf_op | source)
XLA Modules:
  0.0 632.5 jit_solution(2512236024374545083)
XLA Ops:
  8.8 158.2 %fusion = f32[8,768]{1,0:T(8,128)} fusion(f32[384,768]{1,0:T(8,128)S(1)} %fusion.28), kind=kCustom, calls=%all-reduce-scatter | all-reduce-scatter fusion | flops 393217 | bytes 1206272
  167.0 1.9 collective-permute-start.20
  168.9 1.9 collective-permute-start.19
  170.8 1.9 collective-permute-start.18
  172.7 1.9 collective-permute-start.17
  181.1 98.5 %all_gather.3 = bf16[2,256,384]{2,0,1:T(2,128)(2,1)S(1)} all-gather(bf16[2,4,384]{2,0,1:T(2,128)(2,1)S(1)} %copy.1023), channel_id=1, replica_groups=mesh['dp'=8,'seq'=64] {'seq'}, dimensions={1}, use_global_device_ids=true | all-gather | bytes 399360 | tf_op jit(solution)/shard_map/all_gather | solution.py:129
  288.9 2.1 collective-permute-start
  295.6 1.8 multiply_convert_fusion
  298.7 3.0 collective-permute-start.21
  303.2 4.5 collective-permute-start.16
  307.8 9.6 %collective-permute-start.15 = (f32[8,768]{1,0:T(8,128)}, f32[8,768]{1,0:T(8,128)S(1)}, u32[]{:S(2)}, u32[]{:S(2)}) collective-permute-start(f32[8,768]{1,0:T(8,128)} %fusion), channel_id=1, source_target_pairs={{0,10},{1,11},{2,12},{3,13},{4,14},{5,15},{6,16},{7,17},{8,18},{9,... | collective-permute-start | bytes 73736
  317.4 2.6 collective-permute-start.1
  320.7 7.0 %collective-permute-start.14 = (f32[8,768]{1,0:T(8,128)}, f32[8,768]{1,0:T(8,128)S(1)}, u32[]{:S(2)}, u32[]{:S(2)}) collective-permute-start(f32[8,768]{1,0:T(8,128)} %fusion), channel_id=1, source_target_pairs={{0,9},{1,10},{2,11},{3,12},{4,13},{5,14},{6,15},{7,16},{8,17},{9,1... | collective-permute-start | bytes 73736
  327.7 7.8 %collective-permute-start.13 = (f32[8,768]{1,0:T(8,128)}, f32[8,768]{1,0:T(8,128)S(1)}, u32[]{:S(2)}, u32[]{:S(2)}) collective-permute-start(f32[8,768]{1,0:T(8,128)} %fusion), channel_id=1, source_target_pairs={{0,8},{1,9},{2,10},{3,11},{4,12},{5,13},{6,14},{7,15},{8,16},{9,17... | collective-permute-start | bytes 73736
  335.5 4.9 collective-permute-start.12
  340.4 8.4 %collective-permute-start.11 = (f32[8,768]{1,0:T(8,128)}, f32[8,768]{1,0:T(8,128)S(1)}, u32[]{:S(2)}, u32[]{:S(2)}) collective-permute-start(f32[8,768]{1,0:T(8,128)} %fusion), channel_id=1, source_target_pairs={{0,6},{1,7},{2,8},{3,9},{4,10},{5,11},{6,12},{7,13},{8,14},{9,15},... | collective-permute-start | bytes 73736
  348.9 6.3 collective-permute-start.10
  355.3 4.4 collective-permute-start.9
  359.7 3.4 collective-permute-start.8
  363.2 2.2 collective-permute-start.7
  365.3 4.8 collective-permute-start.6
  370.2 2.1 collective-permute-start.2
  373.5 2.3 copy.1056
  375.8 2.4 reshape.1814
  380.2 23.5 %concatenate.120 = f32[134,768]{1,0:T(8,128)} concatenate(f32[6,768]{1,0:T(8,128)S(1)} %copy-done.23, f32[8,768]{1,0:T(8,128)} %collective-permute-done.20, f32[8,768]{1,0:T(8,128)} %collective-permute-done.19, f32[8,768]{1,0:T(8,128)} %collective-permute-done.18, f32[8,768]{1,0:T(8,128)} %collective-permute-done.17, f32[8,768]{1,0:T(8,128)S(1)} %copy-done.25, ...), dimensions={0} | concatenate | bytes 823296
  404.5 21.8 %psum.8 = f32[6,768]{1,0:T(8,128)} all-reduce(f32[6,768]{1,0:T(8,128)S(1)} %constant_dynamic-slice_fusion), channel_id=1, replica_groups=mesh['dp'=8,'seq'=64] {'dp'}, use_global_device_ids=true, to_apply=%region_2.0 | all-reduce | flops 4608 | bytes 36864 | tf_op jit(solution)/shard_map/psum | solution.py:91
  428.4 1.7 copy.1000
  430.2 1.7 copy.983
  433.0 1.9 fusion.32
  439.3 1.9 copy.1057
  441.3 1.8 broadcast_select_fusion
  443.1 7.5 %collective-permute-start.3 = (f32[2,128,384]{2,1,0:T(8,128)}, f32[2,128,384]{2,1,0:T(8,128)}, u32[]{:S(2)}, u32[]{:S(2)}) collective-permute-start(f32[2,128,384]{2,1,0:T(8,128)} %broadcast_select_fusion), channel_id=1, source_target_pairs={{0,4},{1,5},{2,6},{3,7},{4,0},{5,1},{6,2},{7,3},{8,12},{9,13},{10,... | collective-permute-start | bytes 1179656 | tf_op jit(solution)/shard_map/ppermute | solution.py:10
  450.8 1.6 copy.1001
  452.5 2.3 copy.1002
  454.8 2.6 fusion.12
  457.4 1.7 copy.1067
  459.2 24.2 %collective-permute-done.3 = f32[2,128,384]{2,1,0:T(8,128)} collective-permute-done((f32[2,128,384]{2,1,0:T(8,128)}, f32[2,128,384]{2,1,0:T(8,128)}, u32[]{:S(2)}, u32[]{:S(2)}) %collective-permute-start.3) | collective-permute-done | bytes 393248 | tf_op jit(solution)/shard_map/ppermute | solution.py:10
  486.1 1.9 collective-permute-start.4
  488.0 97.0 %all-reduce.11.cloned.1.call-done = f32[2,256,384]{2,1,0:T(8,128)} async-done(((f32[2,256,384]{2,1,0:T(8,128)}), f32[2,256,384]{2,1,0:T(8,128)}) %all-reduce.11.cloned.1.call-update) | async-done | bytes 786448
  591.3 2.3 copy.1063
  593.6 2.4 reshape.1832
  602.5 2.7 collective-permute-start.5
  605.7 2.3 copy.1066
  608.0 2.3 reshape.1850
  612.7 2.3 copy.1060
  616.8 2.3 copy.1065
  619.2 2.4 fusion.11
  621.6 1.7 copy.1068
  (388 shorter events, 57.6 us)
Async XLA Ops:
  7.2 168.7 %copy-start = (bf16[384,768]{1,0:T(8,128)(2,1)S(1)}, bf16[384,768]{1,0:T(8,128)(2,1)}, u32[]{:S(2)}) copy-start(bf16[384,768]{1,0:T(8,128)(2,1)} %param.109) | copy-start | bytes 1769476
  7.2 168.7 %copy-start.7 = (bf16[1,256,768]{2,1,0:T(8,128)(2,1)S(1)}, bf16[1,256,768]{2,1,0:T(8,128)(2,1)}, u32[]{:S(2)}) copy-start(bf16[1,256,768]{2,1,0:T(8,128)(2,1)} %param.107) | copy-start | bytes 1179652
  7.2 167.4 %copy-start.9 = (bf16[1,256,384]{2,1,0:T(8,128)(2,1)S(1)}, bf16[1,256,384]{2,1,0:T(8,128)(2,1)}, u32[]{:S(2)}) copy-start(bf16[1,256,384]{2,1,0:T(8,128)(2,1)} %param.106) | copy-start | bytes 589828
  7.2 167.5 %copy-start.19 = (f32[1,256,8]{1,2,0:T(8,128)S(1)}, f32[1,256,8]{1,2,0:T(8,128)}, u32[]{:S(2)}) copy-start(f32[1,256,8]{1,2,0:T(8,128)} %param.108) | copy-start | bytes 24580
  7.2 169.2 %copy-start.13 = (bf16[1,256,384]{2,1,0:T(8,128)(2,1)S(1)}, bf16[1,256,384]{2,1,0:T(8,128)(2,1)}, u32[]{:S(2)}) copy-start(bf16[1,256,384]{2,1,0:T(8,128)(2,1)} %param.103) | copy-start | bytes 589828
  7.2 577.7 %all-reduce.11.cloned.1.call-start = ((), (), s32[]{:S(2)}) async-start(), calls=%async_computation | async-start | bytes 1572864
  8.8 167.8 %copy-start.10 = (bf16[1,256,384]{2,1,0:T(8,128)(2,1)S(1)}, bf16[1,256,384]{2,1,0:T(8,128)(2,1)}, u32[]{:S(2)}) copy-start(bf16[1,256,384]{2,1,0:T(8,128)(2,1)} %param.104) | copy-start | bytes 589828
  8.8 167.9 %copy-start.11 = (bf16[1,256,384]{2,1,0:T(8,128)(2,1)S(1)}, bf16[1,256,384]{2,1,0:T(8,128)(2,1)}, u32[]{:S(2)}) copy-start(bf16[1,256,384]{2,1,0:T(8,128)(2,1)} %param.105) | copy-start | bytes 589828
  167.0 140.7 %collective-permute-start.20 = (f32[8,768]{1,0:T(8,128)}, f32[8,768]{1,0:T(8,128)}, u32[]{:S(2)}, u32[]{:S(2)}) collective-permute-start(f32[8,768]{1,0:T(8,128)} %fusion), channel_id=1, source_target_pairs={{0,15},{1,16},{2,17},{3,18},{4,19},{5,20},{6,21},{7,22},{8,23},{9,... | collective-permute-start | bytes 73736
  168.9 148.5 %collective-permute-start.19 = (f32[8,768]{1,0:T(8,128)}, f32[8,768]{1,0:T(8,128)}, u32[]{:S(2)}, u32[]{:S(2)}) collective-permute-start(f32[8,768]{1,0:T(8,128)} %fusion), channel_id=1, source_target_pairs={{0,14},{1,15},{2,16},{3,17},{4,18},{5,19},{6,20},{7,21},{8,22},{9,... | collective-permute-start | bytes 73736
  170.8 149.9 %collective-permute-start.18 = (f32[8,768]{1,0:T(8,128)}, f32[8,768]{1,0:T(8,128)}, u32[]{:S(2)}, u32[]{:S(2)}) collective-permute-start(f32[8,768]{1,0:T(8,128)} %fusion), channel_id=1, source_target_pairs={{0,13},{1,14},{2,15},{3,16},{4,17},{5,18},{6,19},{7,20},{8,21},{9,... | collective-permute-start | bytes 73736
  172.7 155.0 %collective-permute-start.17 = (f32[8,768]{1,0:T(8,128)}, f32[8,768]{1,0:T(8,128)}, u32[]{:S(2)}, u32[]{:S(2)}) collective-permute-start(f32[8,768]{1,0:T(8,128)} %fusion), channel_id=1, source_target_pairs={{0,12},{1,13},{2,14},{3,15},{4,16},{5,17},{6,18},{7,19},{8,20},{9,... | collective-permute-start | bytes 73736
  176.7 118.3 %copy-start.4 = (bf16[1,256,384]{1,2,0:T(8,128)(2,1)}, bf16[1,256,384]{1,2,0:T(8,128)(2,1)S(1)}, u32[]{:S(2)}) copy-start(bf16[1,256,384]{1,2,0:T(8,128)(2,1)S(1)} %copy.977) | copy-start | bytes 589828
  288.9 9.8 %collective-permute-start = (bf16[2,32,384]{2,1,0:T(8,128)(2,1)}, bf16[2,32,384]{2,1,0:T(8,128)(2,1)}, u32[]{:S(2)}, u32[]{:S(2)}) collective-permute-start(bf16[2,32,384]{2,1,0:T(8,128)(2,1)} %constant_dynamic-update-slice_fusion.16), channel_id=1, source_target_pairs={{0,1},{1,0},{2,3},{3,2},{4,5},{5,4},{6,7},{7,6},{8,9},{9,8},{10,11... | collective-permute-start | bytes 147464 | tf_op jit(solution)/shard_map/ppermute | solution.py:10
  295.6 24.5 %copy-start.42 = (f32[32]{0:T(128)S(1)}, f32[32]{0:T(128)}, u32[]{:S(2)}) copy-start(f32[32]{0:T(128)} %get-tuple-element.625) | copy-start | bytes 388
  297.4 80.8 %copy-start.43 = (u32[512]{0:T(512)S(1)}, u32[512]{0:T(512)}, u32[]{:S(2)}) copy-start(u32[512]{0:T(512)} %constant.1136) | copy-start | bytes 6148
  298.7 4.5 collective-permute-start.21
  303.2 14.2 %copy-start.22 = (f32[6,768]{1,0:T(8,128)}, f32[6,768]{1,0:T(8,128)S(1)}, u32[]{:S(2)}) copy-start(f32[6,768]{1,0:T(8,128)S(1)} %collective-permute-done.21) | copy-start | bytes 55300
  303.2 32.2 %collective-permute-start.16 = (f32[8,768]{1,0:T(8,128)}, f32[8,768]{1,0:T(8,128)S(1)}, u32[]{:S(2)}, u32[]{:S(2)}) collective-permute-start(f32[8,768]{1,0:T(8,128)} %fusion), channel_id=1, source_target_pairs={{0,11},{1,12},{2,13},{3,14},{4,15},{5,16},{6,17},{7,18},{8,19},{9,... | collective-permute-start | bytes 73736
  307.8 32.6 %collective-permute-start.15 = (f32[8,768]{1,0:T(8,128)}, f32[8,768]{1,0:T(8,128)S(1)}, u32[]{:S(2)}, u32[]{:S(2)}) collective-permute-start(f32[8,768]{1,0:T(8,128)} %fusion), channel_id=1, source_target_pairs={{0,10},{1,11},{2,12},{3,13},{4,14},{5,15},{6,16},{7,17},{8,18},{9,... | collective-permute-start | bytes 73736
  317.4 31.4 %collective-permute-start.1 = (bf16[2,64,384]{2,1,0:T(8,128)(2,1)S(1)}, bf16[2,64,384]{2,1,0:T(8,128)(2,1)S(1)}, u32[]{:S(2)}, u32[]{:S(2)}) collective-permute-start(bf16[2,64,384]{2,1,0:T(8,128)(2,1)S(1)} %maximum_select_fusion.2), channel_id=1, source_target_pairs={{0,2},{1,3},{2,0},{3,1},{4,6},{5,7},{6,4},{7,5},{8,10},{9,11},{10,... | collective-permute-start | bytes 294920 | tf_op jit(solution)/shard_map/ppermute | solution.py:10
  320.7 34.6 %collective-permute-start.14 = (f32[8,768]{1,0:T(8,128)}, f32[8,768]{1,0:T(8,128)S(1)}, u32[]{:S(2)}, u32[]{:S(2)}) collective-permute-start(f32[8,768]{1,0:T(8,128)} %fusion), channel_id=1, source_target_pairs={{0,9},{1,10},{2,11},{3,12},{4,13},{5,14},{6,15},{7,16},{8,17},{9,1... | collective-permute-start | bytes 73736
  327.7 32.0 %collective-permute-start.13 = (f32[8,768]{1,0:T(8,128)}, f32[8,768]{1,0:T(8,128)S(1)}, u32[]{:S(2)}, u32[]{:S(2)}) collective-permute-start(f32[8,768]{1,0:T(8,128)} %fusion), channel_id=1, source_target_pairs={{0,8},{1,9},{2,10},{3,11},{4,12},{5,13},{6,14},{7,15},{8,16},{9,17... | collective-permute-start | bytes 73736
  335.4 13.4 %copy-start.24 = (f32[8,768]{1,0:T(8,128)}, f32[8,768]{1,0:T(8,128)S(1)}, u32[]{:S(2)}) copy-start(f32[8,768]{1,0:T(8,128)S(1)} %collective-permute-done.16) | copy-start | bytes 73732
  335.5 27.7 %collective-permute-start.12 = (f32[8,768]{1,0:T(8,128)}, f32[8,768]{1,0:T(8,128)S(1)}, u32[]{:S(2)}, u32[]{:S(2)}) collective-permute-start(f32[8,768]{1,0:T(8,128)} %fusion), channel_id=1, source_target_pairs={{0,7},{1,8},{2,9},{3,10},{4,11},{5,12},{6,13},{7,14},{8,15},{9,16}... | collective-permute-start | bytes 73736
  340.4 8.4 %copy-start.26 = (f32[8,768]{1,0:T(8,128)}, f32[8,768]{1,0:T(8,128)S(1)}, u32[]{:S(2)}) copy-start(f32[8,768]{1,0:T(8,128)S(1)} %collective-permute-done.15) | copy-start | bytes 73732
  340.4 24.9 %collective-permute-start.11 = (f32[8,768]{1,0:T(8,128)}, f32[8,768]{1,0:T(8,128)S(1)}, u32[]{:S(2)}, u32[]{:S(2)}) collective-permute-start(f32[8,768]{1,0:T(8,128)} %fusion), channel_id=1, source_target_pairs={{0,6},{1,7},{2,8},{3,9},{4,10},{5,11},{6,12},{7,13},{8,14},{9,15},... | collective-permute-start | bytes 73736
  348.9 21.3 %collective-permute-start.10 = (f32[8,768]{1,0:T(8,128)}, f32[8,768]{1,0:T(8,128)S(1)}, u32[]{:S(2)}, u32[]{:S(2)}) collective-permute-start(f32[8,768]{1,0:T(8,128)} %fusion), channel_id=1, source_target_pairs={{0,5},{1,6},{2,7},{3,8},{4,9},{5,10},{6,11},{7,12},{8,13},{9,14},{... | collective-permute-start | bytes 73736
  355.2 71.1 %copy-start.15 = (bf16[2,128,384]{2,1,0:T(8,128)(2,1)}, bf16[2,128,384]{2,1,0:T(8,128)(2,1)S(1)}, u32[]{:S(2)}) copy-start(bf16[2,128,384]{2,1,0:T(8,128)(2,1)S(1)} %maximum_select_fusion.1) | copy-start | bytes 589828
  355.2 24.9 %copy-start.23 = (f32[6,768]{1,0:T(8,128)S(1)}, f32[6,768]{1,0:T(8,128)}, u32[]{:S(2)}) copy-start(f32[6,768]{1,0:T(8,128)} %copy-done.22) | copy-start | bytes 55300
  355.2 24.9 %copy-start.25 = (f32[8,768]{1,0:T(8,128)S(1)}, f32[8,768]{1,0:T(8,128)}, u32[]{:S(2)}) copy-start(f32[8,768]{1,0:T(8,128)} %copy-done.24) | copy-start | bytes 73732
  355.3 24.9 %copy-start.27 = (f32[8,768]{1,0:T(8,128)S(1)}, f32[8,768]{1,0:T(8,128)}, u32[]{:S(2)}) copy-start(f32[8,768]{1,0:T(8,128)} %copy-done.26) | copy-start | bytes 73732
  355.3 14.9 %copy-start.28 = (f32[8,768]{1,0:T(8,128)}, f32[8,768]{1,0:T(8,128)S(1)}, u32[]{:S(2)}) copy-start(f32[8,768]{1,0:T(8,128)S(1)} %collective-permute-done.14) | copy-start | bytes 73732
  355.3 24.8 %collective-permute-start.9 = (f32[8,768]{1,0:T(8,128)}, f32[8,768]{1,0:T(8,128)}, u32[]{:S(2)}, u32[]{:S(2)}) collective-permute-start(f32[8,768]{1,0:T(8,128)} %fusion), channel_id=1, source_target_pairs={{0,4},{1,5},{2,6},{3,7},{4,8},{5,9},{6,10},{7,11},{8,12},{9,13},{1... | collective-permute-start | bytes 73736
  359.7 10.5 %copy-start.30 = (f32[8,768]{1,0:T(8,128)}, f32[8,768]{1,0:T(8,128)S(1)}, u32[]{:S(2)}) copy-start(f32[8,768]{1,0:T(8,128)S(1)} %collective-permute-done.13) | copy-start | bytes 73732
  359.7 20.4 %collective-permute-start.8 = (f32[8,768]{1,0:T(8,128)}, f32[8,768]{1,0:T(8,128)}, u32[]{:S(2)}, u32[]{:S(2)}) collective-permute-start(f32[8,768]{1,0:T(8,128)} %fusion), channel_id=1, source_target_pairs={{0,3},{1,4},{2,5},{3,6},{4,7},{5,8},{6,9},{7,10},{8,11},{9,12},{10... | collective-permute-start | bytes 73736
  363.2 9.1 %copy-start.32 = (f32[8,768]{1,0:T(8,128)}, f32[8,768]{1,0:T(8,128)S(1)}, u32[]{:S(2)}) copy-start(f32[8,768]{1,0:T(8,128)S(1)} %collective-permute-done.12) | copy-start | bytes 73732
  363.2 16.9 %collective-permute-start.7 = (f32[8,768]{1,0:T(8,128)}, f32[8,768]{1,0:T(8,128)}, u32[]{:S(2)}, u32[]{:S(2)}) collective-permute-start(f32[8,768]{1,0:T(8,128)} %fusion), channel_id=1, source_target_pairs={{0,2},{1,3},{2,4},{3,5},{4,6},{5,7},{6,8},{7,9},{8,10},{9,11},{10,... | collective-permute-start | bytes 73736
  365.3 14.8 %collective-permute-start.6 = (f32[8,768]{1,0:T(8,128)}, f32[8,768]{1,0:T(8,128)}, u32[]{:S(2)}, u32[]{:S(2)}) collective-permute-start(f32[8,768]{1,0:T(8,128)} %fusion), channel_id=1, source_target_pairs={{0,1},{1,2},{2,3},{3,4},{4,5},{5,6},{6,7},{7,8},{8,9},{9,10},{10,1... | collective-permute-start | bytes 73736
  370.2 9.9 %copy-start.29 = (f32[8,768]{1,0:T(8,128)S(1)}, f32[8,768]{1,0:T(8,128)}, u32[]{:S(2)}) copy-start(f32[8,768]{1,0:T(8,128)} %copy-done.28) | copy-start | bytes 73732
  370.2 56.1 %collective-permute-start.2 = (bf16[2,128,384]{2,1,0:T(8,128)(2,1)S(1)}, bf16[2,128,384]{2,1,0:T(8,128)(2,1)}, u32[]{:S(2)}, u32[]{:S(2)}) collective-permute-start(bf16[2,128,384]{2,1,0:T(8,128)(2,1)S(1)} %maximum_select_fusion.1), channel_id=1, source_target_pairs={{0,4},{1,5},{2,6},{3,7},{4,0},{5,1},{6,2},{7,3},{8,12},{9,13},{10,... | collective-permute-start | bytes 589832 | tf_op jit(solution)/shard_map/ppermute | solution.py:10
  375.8 56.1 %copy-start.41 = (f32[32,8,1]{0,2,1:T(1,128)S(1)}, f32[32,8,1]{0,2,1:T(1,128)}, u32[]{:S(2)}) copy-start(f32[32,8,1]{0,2,1:T(1,128)} %copy-done.40) | copy-start | bytes 3076
  380.1 54.8 %copy-start.39 = (f32[32,8,1]{0,2,1:T(1,128)S(1)}, f32[32,8,1]{0,2,1:T(1,128)}, u32[]{:S(2)}) copy-start(f32[32,8,1]{0,2,1:T(1,128)} %constant_dynamic-update-slice_fusion.42) | copy-start | bytes 3076
  441.3 9.5 %copy-start.17 = (f32[32,8,48]{2,0,1:T(8,128)S(1)}, f32[32,8,48]{2,0,1:T(8,128)}, u32[]{:S(2)}) copy-start(f32[32,8,48]{2,0,1:T(8,128)} %copy-done.16) | copy-start | bytes 147460
  443.1 40.3 %collective-permute-start.3 = (f32[2,128,384]{2,1,0:T(8,128)}, f32[2,128,384]{2,1,0:T(8,128)}, u32[]{:S(2)}, u32[]{:S(2)}) collective-permute-start(f32[2,128,384]{2,1,0:T(8,128)} %broadcast_select_fusion), channel_id=1, source_target_pairs={{0,4},{1,5},{2,6},{3,7},{4,0},{5,1},{6,2},{7,3},{8,12},{9,13},{10,... | collective-permute-start | bytes 1179656 | tf_op jit(solution)/shard_map/ppermute | solution.py:10
  486.1 114.7 %collective-permute-start.4 = (f32[2,64,384]{2,1,0:T(8,128)}, f32[2,64,384]{2,1,0:T(8,128)}, u32[]{:S(2)}, u32[]{:S(2)}) collective-permute-start(f32[2,64,384]{2,1,0:T(8,128)} %slice_select_fusion), channel_id=1, source_target_pairs={{0,2},{1,3},{2,0},{3,1},{4,6},{5,7},{6,4},{7,5},{8,10},{9,11},{10,... | collective-permute-start | bytes 589832 | tf_op jit(solution)/shard_map/ppermute | solution.py:10
  587.2 13.6 %copy-start.3 = (f32[2,128,384]{2,1,0:T(8,128)S(1)}, f32[2,128,384]{2,1,0:T(8,128)}, u32[]{:S(2)}) copy-start(f32[2,128,384]{2,1,0:T(8,128)} %copy-done.2) | copy-start | bytes 1179652
  602.5 7.9 %collective-permute-start.5 = (f32[2,32,384]{2,1,0:T(8,128)S(1)}, f32[2,32,384]{2,1,0:T(8,128)S(1)}, u32[]{:S(2)}, u32[]{:S(2)}) collective-permute-start(f32[2,32,384]{2,1,0:T(8,128)S(1)} %slice_select_fusion.1), channel_id=1, source_target_pairs={{0,1},{1,0},{2,3},{3,2},{4,5},{5,4},{6,7},{7,6},{8,9},{9,8},{10,11... | collective-permute-start | bytes 294920 | tf_op jit(solution)/shard_map/ppermute | solution.py:10
  (19 other events, 73.6 us)
Sparse Core Ops, SparseCore 0:
  286.1 298.8 all-reduce.10
where the time goes:
time: 636 us; the launch traced here: 633 us
  blocking collectives  279 us (44%)
  waiting for transfers between devices  122 us (19%)
  local copies, waits for them, and re-layouts  96.5 us (15%)
  starting transfers between devices  92.8 us (15%)
  matrix products  17.9 us (3%)
  between operations  16.9 us (3%)
  other arithmetic  8.05 us (1%)
    unnamed x1, blocking collectives  158 us
    all_gather x1, blocking collectives, on_device(): far_remote = lax.all_gather(far_pair, 'seq', axis=1, tiled=True)  98.5 us
    unnamed x18, waiting for transfers between devices  97.6 us
    unnamed x17, starting transfers between devices  74 us
    unnamed x208, local copies, waits for them, and re-layouts  38 us
    ppermute x6, waiting for transfers between devices, swapped(): lax.ppermute(shard, axis, [(i, i ^ 1 << distance) for i in range(lax.axis...  24.2 us
    scatter x54, local copies, waits for them, and re-layouts, place(): shaped = shaped.at[:, h % stride, h, :].set(y[:, h, :])  23.4 us
    psum x1, blocking collectives, on_device(): summed = lax.psum(full, 'dp')  21.8 us
  transfers between devices with their start and end apart: 23, of which 3 were waited for; matrix products, arithmetic and copies ran while one was open for 16% of the time, Pallas kernels for 0%

commit v1 on v0

--- a/solution.py
+++ b/solution.py
@@ -88,7 +88,9 @@
     full = lax.dot_general(
         output2, upstream, (((0,), (0,)), ((), ())), preferred_element_type=jnp.float32
     )
-    summed = lax.psum(full, "dp")
+    summed = full
+    for hop in (1, 2, 4):
+        summed = summed + lax.ppermute(summed, "dp", [(dev, dev ^ hop) for dev in range(8)])
     grad_weight = lax.psum_scatter(summed, "seq", scatter_dimension=0, tiled=True)
     dq0, dk0, dv0 = set_backward(query3, dout3, lse, delta, key3, value3, scale)
     total_q = dq0

time: 636 us -> 727 us (1.14)
  the two profiles are of different devices: /device:TPU:8 before, /device:TPU:32 now
where the time goes in v1:
time: 727 us; the launch traced here: 725 us
  blocking collectives  250 us (34%)
  waiting for transfers between devices  240 us (33%)
  starting transfers between devices  101 us (14%)
  local copies, waits for them, and re-layouts  83.8 us (12%)
  matrix products  18.3 us (3%)
  between operations  16.8 us (2%)
  other arithmetic  14.3 us (2%)
    unnamed x18, waiting for transfers between devices  180 us
    unnamed x1, blocking collectives  151 us
    all_gather x1, blocking collectives, on_device(): far_remote = lax.all_gather(far_pair, 'seq', axis=1, tiled=True)  99.4 us
    unnamed x17, starting transfers between devices  63.3 us
    ppermute x6, waiting for transfers between devices, swapped(): lax.ppermute(shard, axis, [(i, i ^ 1 << distance) for i in range(lax.axis...  38 us
    scatter x54, local copies, waits for them, and re-layouts, place(): shaped = shaped.at[:, h % stride, h, :].set(y[:, h, :])  28.5 us
    ppermute x6, starting transfers between devices, swapped(): lax.ppermute(shard, axis, [(i, i ^ 1 << distance) for i in range(lax.axis...  26.4 us
    ppermute x3, waiting for transfers between devices, on_device(): lax.ppermute(summed, 'dp', [(dev, dev ^ hop) for dev in range(8)])  21.7 us
  transfers between devices with their start and end apart: 26, of which 6 were waited for; matrix products, arithmetic and copies ran while one was open for 13% of the time, Pallas kernels for 0%

profile of v1, /device:TPU:32, one launch (start us, length us, event | category | flops | bytes accessed | tf_op | source)
XLA Modules:
  0.0 724.9 jit_solution(1172852382626350500)
XLA Ops:
  16.5 99.4 %all_gather.3 = bf16[2,256,384]{2,0,1:T(2,128)(2,1)S(1)} all-gather(bf16[2,4,384]{2,0,1:T(2,128)(2,1)S(1)} %copy.1023), channel_id=1, replica_groups=mesh['dp'=8,'seq'=64] {'seq'}, dimensions={1}, use_global_device_ids=true | all-gather | bytes 399360 | tf_op jit(solution)/shard_map/all_gather | solution.py:131
  127.1 3.9 collective-permute-start
  132.4 1.9 collective-permute-start.6
  141.5 1.8 multiply_convert_fusion
  144.7 3.7 collective-permute-start.1
  149.7 2.3 copy.1056
  152.0 2.4 reshape.1814
  156.3 4.5 collective-permute-start.2
  161.4 16.7 %collective-permute-done.2 = bf16[2,128,384]{2,1,0:T(8,128)(2,1)S(1)} collective-permute-done((bf16[2,128,384]{2,1,0:T(8,128)(2,1)S(1)}, bf16[2,128,384]{2,1,0:T(8,128)(2,1)S(1)}, u32[]{:S(2)}, u32[]{:S(2)}) %collective-permute-start.2) | collective-permute-done | bytes 196640 | tf_op jit(solution)/shard_map/ppermute | solution.py:10
  179.0 1.7 copy.1000
  180.7 1.7 copy.983
  183.6 1.8 fusion.32
  189.8 1.9 copy.1057
  191.7 1.8 broadcast_select_fusion
  193.6 1.9 collective-permute-start.3
  195.7 1.6 copy.1001
  197.3 2.3 copy.1002
  199.6 2.6 fusion.12
  202.3 1.7 copy.1067
  204.0 21.3 %collective-permute-done.3 = f32[2,128,384]{2,1,0:T(8,128)} collective-permute-done((f32[2,128,384]{2,1,0:T(8,128)}, f32[2,128,384]{2,1,0:T(8,128)}, u32[]{:S(2)}, u32[]{:S(2)}) %collective-permute-start.3) | collective-permute-done | bytes 393248 | tf_op jit(solution)/shard_map/ppermute | solution.py:10
  227.9 9.1 %collective-permute-start.4 = (f32[2,64,384]{2,1,0:T(8,128)}, f32[2,64,384]{2,1,0:T(8,128)}, u32[]{:S(2)}, u32[]{:S(2)}) collective-permute-start(f32[2,64,384]{2,1,0:T(8,128)} %slice_select_fusion), channel_id=1, source_target_pairs={{0,2},{1,3},{2,0},{3,1},{4,6},{5,7},{6,4},{7,5},{8,10},{9,11},{10,... | collective-permute-start | bytes 589832 | tf_op jit(solution)/shard_map/ppermute | solution.py:10
  237.0 180.1 %all-reduce.11.cloned.1.call-done = f32[2,256,384]{2,1,0:T(8,128)} async-done(((f32[2,256,384]{2,1,0:T(8,128)}), f32[2,256,384]{2,1,0:T(8,128)}) %all-reduce.11.cloned.1.call-update) | async-done | bytes 786448
  425.1 2.3 copy.1063
  427.4 2.4 reshape.1832
  434.4 3.3 collective-permute-start.5
  438.2 2.3 copy.1066
  440.6 2.4 reshape.1850
  443.0 2.8 add.157
  445.8 3.4 collective-permute-start.7
  451.5 15.9 %collective-permute-done.7 = f32[384,768]{1,0:T(8,128)} collective-permute-done((f32[384,768]{1,0:T(8,128)}, f32[384,768]{1,0:T(8,128)}, u32[]{:S(2)}, u32[]{:S(2)}) %collective-permute-start.7) | collective-permute-done | bytes 1179680 | tf_op jit(solution)/shard_map/ppermute | solution.py:93
  467.4 2.8 add.158
  470.2 6.0 collective-permute-start.8
  477.9 2.3 copy.1065
  484.8 2.2 fusion.10
  487.0 5.9 collective-permute-done.8
  492.9 1.8 add.159
  494.6 151.1 %fusion = f32[8,768]{1,0:T(8,128)S(1)} fusion(f32[384,768]{1,0:T(8,128)S(1)} %add.159), kind=kCustom, calls=%all-reduce-scatter | all-reduce-scatter fusion | flops 393217 | bytes 1206272
  649.8 4.5 collective-permute-start.21
  657.0 16.0 %collective-permute-start.18 = (f32[8,768]{1,0:T(8,128)S(1)}, f32[8,768]{1,0:T(8,128)S(1)}, u32[]{:S(2)}, u32[]{:S(2)}) collective-permute-start(f32[8,768]{1,0:T(8,128)S(1)} %fusion), channel_id=1, source_target_pairs={{0,10},{1,11},{2,12},{3,13},{4,14},{5,15},{6,16},{7,17},{8,18},{9,... | collective-permute-start | bytes 73736
  673.0 1.9 collective-permute-start.17
  674.9 1.9 collective-permute-start.16
  676.9 11.2 %collective-permute-start.15 = (f32[8,768]{1,0:T(8,128)S(1)}, f32[8,768]{1,0:T(8,128)S(1)}, u32[]{:S(2)}, u32[]{:S(2)}) collective-permute-start(f32[8,768]{1,0:T(8,128)S(1)} %fusion), channel_id=1, source_target_pairs={{0,7},{1,8},{2,9},{3,10},{4,11},{5,12},{6,13},{7,14},{8,15},{9,16}... | collective-permute-start | bytes 73736
  692.6 6.3 collective-permute-start.13
  698.9 4.9 collective-permute-start.12
  703.8 1.6 collective-permute-start.11
  705.5 4.5 collective-permute-start.10
  710.0 2.5 collective-permute-start.9
  715.7 1.7 concatenate.120
  (360 shorter events, 77.8 us)
Async XLA Ops:
  7.2 2.0 copy-start
  7.2 4.6 copy-start.14
  7.2 4.7 copy-start.15
  7.2 4.9 copy-start.11
  7.2 409.9 %all-reduce.11.cloned.1.call-start = ((), (), s32[]{:S(2)}) async-start(), calls=%async_computation | async-start | bytes 1572864
  11.9 129.0 %copy-start.6 = (bf16[1,256,384]{1,2,0:T(8,128)(2,1)}, bf16[1,256,384]{1,2,0:T(8,128)(2,1)S(1)}, u32[]{:S(2)}) copy-start(bf16[1,256,384]{1,2,0:T(8,128)(2,1)S(1)} %copy.977) | copy-start | bytes 589828
  122.2 8.8 %copy-start.9 = (bf16[1,256,768]{2,1,0:T(8,128)(2,1)S(1)}, bf16[1,256,768]{2,1,0:T(8,128)(2,1)}, u32[]{:S(2)}) copy-start(bf16[1,256,768]{2,1,0:T(8,128)(2,1)} %param.107) | copy-start | bytes 1179652
  122.2 8.8 %copy-start.12 = (bf16[1,256,384]{2,1,0:T(8,128)(2,1)S(1)}, bf16[1,256,384]{2,1,0:T(8,128)(2,1)}, u32[]{:S(2)}) copy-start(bf16[1,256,384]{2,1,0:T(8,128)(2,1)} %param.106) | copy-start | bytes 589828
  123.7 10.7 %copy-start.20 = (f32[1,256,8]{1,2,0:T(8,128)S(1)}, f32[1,256,8]{1,2,0:T(8,128)}, u32[]{:S(2)}) copy-start(f32[1,256,8]{1,2,0:T(8,128)} %param.108) | copy-start | bytes 24580
  125.2 9.9 %copy-start.16 = (bf16[1,256,384]{2,1,0:T(8,128)(2,1)S(1)}, bf16[1,256,384]{2,1,0:T(8,128)(2,1)}, u32[]{:S(2)}) copy-start(bf16[1,256,384]{2,1,0:T(8,128)(2,1)} %param.103) | copy-start | bytes 589828
  127.1 16.7 %collective-permute-start = (bf16[2,32,384]{2,1,0:T(8,128)(2,1)}, bf16[2,32,384]{2,1,0:T(8,128)(2,1)}, u32[]{:S(2)}, u32[]{:S(2)}) collective-permute-start(bf16[2,32,384]{2,1,0:T(8,128)(2,1)} %constant_dynamic-update-slice_fusion.16), channel_id=1, source_target_pairs={{0,1},{1,0},{2,3},{3,2},{4,5},{5,4},{6,7},{7,6},{8,9},{9,8},{10,11... | collective-permute-start | bytes 147464 | tf_op jit(solution)/shard_map/ppermute | solution.py:10
  132.4 310.5 %collective-permute-start.6 = (f32[384,768]{1,0:T(8,128)}, f32[384,768]{1,0:T(8,128)}, u32[]{:S(2)}, u32[]{:S(2)}) collective-permute-start(f32[384,768]{1,0:T(8,128)} %fusion.28), channel_id=1, source_target_pairs={{0,64},{64,0},{128,192},{192,128},{256,320},{320,256},{384,448},{4... | collective-permute-start | bytes 3538952 | tf_op jit(solution)/shard_map/ppermute | solution.py:93
  137.8 2.6 copy-start.2
  137.9 2.6 copy-start.22
  143.3 11.1 %copy-start.25 = (u32[512]{0:T(512)S(1)}, u32[512]{0:T(512)}, u32[]{:S(2)}) copy-start(u32[512]{0:T(512)} %constant.1136) | copy-start | bytes 6148
  143.3 17.5 %copy-start.24 = (f32[32]{0:T(128)S(1)}, f32[32]{0:T(128)}, u32[]{:S(2)}) copy-start(f32[32]{0:T(128)} %get-tuple-element.624) | copy-start | bytes 388
  144.7 11.5 %collective-permute-start.1 = (bf16[2,64,384]{2,1,0:T(8,128)(2,1)S(1)}, bf16[2,64,384]{2,1,0:T(8,128)(2,1)S(1)}, u32[]{:S(2)}, u32[]{:S(2)}) collective-permute-start(bf16[2,64,384]{2,1,0:T(8,128)(2,1)S(1)} %maximum_select_fusion.2), channel_id=1, source_target_pairs={{0,2},{1,3},{2,0},{3,1},{4,6},{5,7},{6,4},{7,5},{8,10},{9,11},{10,... | collective-permute-start | bytes 294920 | tf_op jit(solution)/shard_map/ppermute | solution.py:10
  152.0 30.5 %copy-start.23 = (f32[32,8,1]{0,2,1:T(1,128)S(1)}, f32[32,8,1]{0,2,1:T(1,128)}, u32[]{:S(2)}) copy-start(f32[32,8,1]{0,2,1:T(1,128)} %copy-done.22) | copy-start | bytes 3076
  156.3 21.8 %collective-permute-start.2 = (bf16[2,128,384]{2,1,0:T(8,128)(2,1)S(1)}, bf16[2,128,384]{2,1,0:T(8,128)(2,1)S(1)}, u32[]{:S(2)}, u32[]{:S(2)}) collective-permute-start(bf16[2,128,384]{2,1,0:T(8,128)(2,1)S(1)} %maximum_select_fusion.1), channel_id=1, source_target_pairs={{0,4},{1,5},{2,6},{3,7},{4,0},{5,1},{6,2},{7,3},{8,12},{9,13},{10,... | collective-permute-start | bytes 589832 | tf_op jit(solution)/shard_map/ppermute | solution.py:10
  191.7 3.9 copy-start.18
  193.6 31.7 %collective-permute-start.3 = (f32[2,128,384]{2,1,0:T(8,128)}, f32[2,128,384]{2,1,0:T(8,128)}, u32[]{:S(2)}, u32[]{:S(2)}) collective-permute-start(f32[2,128,384]{2,1,0:T(8,128)} %broadcast_select_fusion), channel_id=1, source_target_pairs={{0,4},{1,5},{2,6},{3,7},{4,0},{5,1},{6,2},{7,3},{8,12},{9,13},{10,... | collective-permute-start | bytes 1179656 | tf_op jit(solution)/shard_map/ppermute | solution.py:10
  227.9 204.8 %collective-permute-start.4 = (f32[2,64,384]{2,1,0:T(8,128)}, f32[2,64,384]{2,1,0:T(8,128)}, u32[]{:S(2)}, u32[]{:S(2)}) collective-permute-start(f32[2,64,384]{2,1,0:T(8,128)} %slice_select_fusion), channel_id=1, source_target_pairs={{0,2},{1,3},{2,0},{3,1},{4,6},{5,7},{6,4},{7,5},{8,10},{9,11},{10,... | collective-permute-start | bytes 589832 | tf_op jit(solution)/shard_map/ppermute | solution.py:10
  419.3 13.4 %copy-start.5 = (f32[2,128,384]{2,1,0:T(8,128)S(1)}, f32[2,128,384]{2,1,0:T(8,128)}, u32[]{:S(2)}) copy-start(f32[2,128,384]{2,1,0:T(8,128)} %copy-done.4) | copy-start | bytes 1179652
  434.4 14.8 %collective-permute-start.5 = (f32[2,32,384]{2,1,0:T(8,128)S(1)}, f32[2,32,384]{2,1,0:T(8,128)S(1)}, u32[]{:S(2)}, u32[]{:S(2)}) collective-permute-start(f32[2,32,384]{2,1,0:T(8,128)S(1)} %slice_select_fusion.1), channel_id=1, source_target_pairs={{0,1},{1,0},{2,3},{3,2},{4,5},{5,4},{6,7},{7,6},{8,9},{9,8},{10,11... | collective-permute-start | bytes 294920 | tf_op jit(solution)/shard_map/ppermute | solution.py:10
  440.6 8.6 %copy-start.8 = (f32[2,64,384]{2,1,0:T(8,128)S(1)}, f32[2,64,384]{2,1,0:T(8,128)}, u32[]{:S(2)}) copy-start(f32[2,64,384]{2,1,0:T(8,128)} %copy-done.7) | copy-start | bytes 589828
  445.8 21.6 %collective-permute-start.7 = (f32[384,768]{1,0:T(8,128)}, f32[384,768]{1,0:T(8,128)}, u32[]{:S(2)}, u32[]{:S(2)}) collective-permute-start(f32[384,768]{1,0:T(8,128)} %add.157), channel_id=1, source_target_pairs={{0,128},{64,192},{128,0},{192,64},{256,384},{320,448},{384,256},{4... | collective-permute-start | bytes 3538952 | tf_op jit(solution)/shard_map/ppermute | solution.py:93
  470.2 13.9 %copy-start.21 = (f32[32,1,48]{2,1,0:T(1,128)S(1)}, f32[32,1,48]{2,1,0:T(1,128)}, u32[]{:S(2)}) copy-start(f32[32,1,48]{2,1,0:T(1,128)} %get-tuple-element.729) | copy-start | bytes 18436
  470.2 14.5 %copy-start.10 = (f32[256,8,48]{0,2,1:T(8,128)S(1)}, f32[256,8,48]{0,2,1:T(8,128)}, u32[]{:S(2)}) copy-start(f32[256,8,48]{0,2,1:T(8,128)} %reshape.1850) | copy-start | bytes 1179652
  470.2 22.6 %collective-permute-start.8 = (f32[384,768]{1,0:T(8,128)}, f32[384,768]{1,0:T(8,128)}, u32[]{:S(2)}, u32[]{:S(2)}) collective-permute-start(f32[384,768]{1,0:T(8,128)} %add.158), channel_id=1, source_target_pairs={{0,256},{64,320},{128,384},{192,448},{256,0},{320,64},{384,128},{4... | collective-permute-start | bytes 3538952 | tf_op jit(solution)/shard_map/ppermute | solution.py:93
  487.0 160.2 %copy-start.3 = (f32[32,8,8,48]{3,0,2,1:T(8,128)S(1)}, f32[32,8,8,48]{3,0,2,1:T(8,128)}, u32[]{:S(2)}) copy-start(f32[32,8,8,48]{3,0,2,1:T(8,128)} %constant_dynamic-update-slice_fusion.122) | copy-start | bytes 1179652
  645.7 66.8 %copy-start.1 = (bf16[8,256,256]{2,1,0:T(8,128)(2,1)S(1)}, bf16[8,256,256]{2,1,0:T(8,128)(2,1)}, u32[]{:S(2)}) copy-start(bf16[8,256,256]{2,1,0:T(8,128)(2,1)} %multiply_convert_fusion) | copy-start | bytes 3145732
  645.8 9.9 %collective-permute-start.24 = (f32[6,768]{1,0:T(8,128)S(1)}, f32[6,768]{1,0:T(8,128)S(1)}, u32[]{:S(2)}, u32[]{:S(2)}) collective-permute-start(f32[6,768]{1,0:T(8,128)S(1)} %slice.2078), channel_id=1, source_target_pairs={{0,16},{1,17},{2,18},{3,19},{4,20},{5,21},{6,22},{7,23},{8,24},{9,... | collective-permute-start | bytes 55304
  647.2 9.8 %collective-permute-start.23 = (f32[8,768]{1,0:T(8,128)S(1)}, f32[8,768]{1,0:T(8,128)S(1)}, u32[]{:S(2)}, u32[]{:S(2)}) collective-permute-start(f32[8,768]{1,0:T(8,128)S(1)} %fusion), channel_id=1, source_target_pairs={{0,15},{1,16},{2,17},{3,18},{4,19},{5,20},{6,21},{7,22},{8,23},{9,... | collective-permute-start | bytes 73736
  648.5 24.5 %collective-permute-start.22 = (f32[8,768]{1,0:T(8,128)S(1)}, f32[8,768]{1,0:T(8,128)S(1)}, u32[]{:S(2)}, u32[]{:S(2)}) collective-permute-start(f32[8,768]{1,0:T(8,128)S(1)} %fusion), channel_id=1, source_target_pairs={{0,14},{1,15},{2,16},{3,17},{4,18},{5,19},{6,20},{7,21},{8,22},{9,... | collective-permute-start | bytes 73736
  649.8 25.1 %collective-permute-start.21 = (f32[8,768]{1,0:T(8,128)S(1)}, f32[8,768]{1,0:T(8,128)S(1)}, u32[]{:S(2)}, u32[]{:S(2)}) collective-permute-start(f32[8,768]{1,0:T(8,128)S(1)} %fusion), channel_id=1, source_target_pairs={{0,13},{1,14},{2,15},{3,16},{4,17},{5,18},{6,19},{7,20},{8,21},{9,... | collective-permute-start | bytes 73736
  654.3 22.5 %collective-permute-start.20 = (f32[8,768]{1,0:T(8,128)S(1)}, f32[8,768]{1,0:T(8,128)S(1)}, u32[]{:S(2)}, u32[]{:S(2)}) collective-permute-start(f32[8,768]{1,0:T(8,128)S(1)} %fusion), channel_id=1, source_target_pairs={{0,12},{1,13},{2,14},{3,15},{4,16},{5,17},{6,18},{7,19},{8,20},{9,... | collective-permute-start | bytes 73736
  655.6 32.4 %collective-permute-start.19 = (f32[8,768]{1,0:T(8,128)S(1)}, f32[8,768]{1,0:T(8,128)S(1)}, u32[]{:S(2)}, u32[]{:S(2)}) collective-permute-start(f32[8,768]{1,0:T(8,128)S(1)} %fusion), channel_id=1, source_target_pairs={{0,11},{1,12},{2,13},{3,14},{4,15},{5,16},{6,17},{7,18},{8,19},{9,... | collective-permute-start | bytes 73736
  657.0 35.6 %collective-permute-start.18 = (f32[8,768]{1,0:T(8,128)S(1)}, f32[8,768]{1,0:T(8,128)S(1)}, u32[]{:S(2)}, u32[]{:S(2)}) collective-permute-start(f32[8,768]{1,0:T(8,128)S(1)} %fusion), channel_id=1, source_target_pairs={{0,10},{1,11},{2,12},{3,13},{4,14},{5,15},{6,16},{7,17},{8,18},{9,... | collective-permute-start | bytes 73736
  673.0 25.9 %collective-permute-start.17 = (f32[8,768]{1,0:T(8,128)S(1)}, f32[8,768]{1,0:T(8,128)S(1)}, u32[]{:S(2)}, u32[]{:S(2)}) collective-permute-start(f32[8,768]{1,0:T(8,128)S(1)} %fusion), channel_id=1, source_target_pairs={{0,9},{1,10},{2,11},{3,12},{4,13},{5,14},{6,15},{7,16},{8,17},{9,1... | collective-permute-start | bytes 73736
  674.9 28.9 %collective-permute-start.16 = (f32[8,768]{1,0:T(8,128)S(1)}, f32[8,768]{1,0:T(8,128)S(1)}, u32[]{:S(2)}, u32[]{:S(2)}) collective-permute-start(f32[8,768]{1,0:T(8,128)S(1)} %fusion), channel_id=1, source_target_pairs={{0,8},{1,9},{2,10},{3,11},{4,12},{5,13},{6,14},{7,15},{8,16},{9,17... | collective-permute-start | bytes 73736
  676.9 28.6 %collective-permute-start.15 = (f32[8,768]{1,0:T(8,128)S(1)}, f32[8,768]{1,0:T(8,128)S(1)}, u32[]{:S(2)}, u32[]{:S(2)}) collective-permute-start(f32[8,768]{1,0:T(8,128)S(1)} %fusion), channel_id=1, source_target_pairs={{0,7},{1,8},{2,9},{3,10},{4,11},{5,12},{6,13},{7,14},{8,15},{9,16}... | collective-permute-start | bytes 73736
  688.1 21.9 %collective-permute-start.14 = (f32[8,768]{1,0:T(8,128)S(1)}, f32[8,768]{1,0:T(8,128)S(1)}, u32[]{:S(2)}, u32[]{:S(2)}) collective-permute-start(f32[8,768]{1,0:T(8,128)S(1)} %fusion), channel_id=1, source_target_pairs={{0,6},{1,7},{2,8},{3,9},{4,10},{5,11},{6,12},{7,13},{8,14},{9,15},... | collective-permute-start | bytes 73736
  691.0 23.6 %copy-start.13 = (bf16[256,8,48]{0,2,1:T(8,128)(2,1)S(1)}, bf16[256,8,48]{0,2,1:T(8,128)(2,1)}, u32[]{:S(2)}) copy-start(bf16[256,8,48]{0,2,1:T(8,128)(2,1)} %fusion.10) | copy-start | bytes 589828
  692.6 22.8 %collective-permute-start.13 = (f32[8,768]{1,0:T(8,128)S(1)}, f32[8,768]{1,0:T(8,128)S(1)}, u32[]{:S(2)}, u32[]{:S(2)}) collective-permute-start(f32[8,768]{1,0:T(8,128)S(1)} %fusion), channel_id=1, source_target_pairs={{0,5},{1,6},{2,7},{3,8},{4,9},{5,10},{6,11},{7,12},{8,13},{9,14},{... | collective-permute-start | bytes 73736
  698.9 16.5 %collective-permute-start.12 = (f32[8,768]{1,0:T(8,128)S(1)}, f32[8,768]{1,0:T(8,128)S(1)}, u32[]{:S(2)}, u32[]{:S(2)}) collective-permute-start(f32[8,768]{1,0:T(8,128)S(1)} %fusion), channel_id=1, source_target_pairs={{0,4},{1,5},{2,6},{3,7},{4,8},{5,9},{6,10},{7,11},{8,12},{9,13},{1... | collective-permute-start | bytes 73736
  703.8 11.6 %collective-permute-start.11 = (f32[8,768]{1,0:T(8,128)S(1)}, f32[8,768]{1,0:T(8,128)S(1)}, u32[]{:S(2)}, u32[]{:S(2)}) collective-permute-start(f32[8,768]{1,0:T(8,128)S(1)} %fusion), channel_id=1, source_target_pairs={{0,3},{1,4},{2,5},{3,6},{4,7},{5,8},{6,9},{7,10},{8,11},{9,12},{10... | collective-permute-start | bytes 73736
  705.5 10.0 %collective-permute-start.10 = (f32[8,768]{1,0:T(8,128)S(1)}, f32[8,768]{1,0:T(8,128)S(1)}, u32[]{:S(2)}, u32[]{:S(2)}) collective-permute-start(f32[8,768]{1,0:T(8,128)S(1)} %fusion), channel_id=1, source_target_pairs={{0,2},{1,3},{2,4},{3,5},{4,6},{5,7},{6,8},{7,9},{8,10},{9,11},{10,... | collective-permute-start | bytes 73736
  710.0 5.7 collective-permute-start.9
  (4 other events, 3.1 us)
Sparse Core Ops, SparseCore 0:
  122.4 294.6 all-reduce.10
